TPU v7x, 32 devices: a whole 2x2x4 slice. The times are simulated.
32 devices in a mesh: member: 2 (over y), gx: 4 (over z), gy: 4 (over x, core).
Axes of the slice: x: 2, y: 2, z: 4, core: 2. Of those that a mesh axis runs over, the one named last changes fastest.
Arguments:
- velocity: float32 [6, 32, 96, 128], P('member', 'gx', 'gy'), parts along dimension 0, may hold values from -6 to 6
- turbine_frame: float32 [4, 4, 8], P('gx', 'gy', 'member'), parts along dimension 2, may hold values from -4 to 128, as said below
- turbine_live: int32 [4, 4, 2], P('gx', 'gy', 'member'), parts along dimension 2, may hold values 0 or 1
- polar_bin: int32 [4, 4, 6, 256], P('gx', 'gy', 'member'), parts along dimension 2, may hold values from 0 to 7
- erosion_id: int32 [4, 4, 6], P('gx', 'gy', 'member'), parts along dimension 2, may hold values from 0 to 15
- polar: float32 [5, 8], replicated, may hold values from 0.01 to 6.5
- erosion: float32 [2, 16], replicated, may hold values from 0.6 to 2
Outputs:
- flow: float32 [6, 32, 96, 128], P('member', 'gx', 'gy'), parts along dimension 0
- blade_load: float32 [4, 4, 6, 3, 256], P('gx', 'gy', 'member'), parts along dimension 2
There are 2 independent parts, one for each index of `member`. A program takes and returns all parts, laid end to end along the dimension named above; an argument that names none is the same for every part. Nothing has to cross between parts.
Inputs may be any that keep to these rules, and one draw needn't show every extreme that they name: turbine_frame holds x in [0, 8), y in [0, 24), z in [8, 120], then an azimuth in [-pi, pi).
All inputs are finite; a program needn't handle non-finite values. No bound on the sum of `turbine_live` on one device may be relied on, other than what follows from the above.
Results may differ from a plain program's by a relative error of at most 0.0003.
The roundings to bfloat16 on the way count: a program that leaves them out, or rounds other values in their place, can miss the bound.
Values sent between devices are 32-bit elements; how exact they have to be, the bound alone decides.
A program may use at most 64 MiB of HBM per device.

v0:
```python
import math

import jax
import jax.numpy as jnp
from jax import lax
from jax.sharding import PartitionSpec as P

PTS = 256
NSEC = 8
NERO = 16
STEPS = 2
RADIUS = 5


TIP_SPEED = 6.0
TIME_STEP = 0.15
BASE_VISCOSITY = 0.1
SMAG_COEF = 0.04
KERNEL_NORM = 35.0 / 96.0
TWIST_RATE = 0.3


def with_halo(cells, sides, width):
    for axis, dim in sides:
        count = lax.axis_size(axis)
        head = lax.slice_in_dim(cells, 0, width, axis=dim)
        tail = lax.slice_in_dim(cells, cells.shape[dim] - width, cells.shape[dim], axis=dim)
        cells = jnp.concatenate(
            [
                lax.ppermute(tail, axis, [(i, (i + 1) % count) for i in range(count)]),
                cells,
                lax.ppermute(head, axis, [((i + 1) % count, i) for i in range(count)]),
            ],
            axis=dim,
        )
    return cells


def kernel(distance):
    inside = jnp.maximum(1.0 - distance * distance / 9.0, 0.0)
    return KERNEL_NORM * inside * inside * inside


def advance(middle, x_plus, x_minus, y_plus, y_minus, push):
    blank_face = jnp.zeros_like(middle[..., :1])
    z_plus = jnp.concatenate([middle[..., 1:], blank_face], axis=-1)
    z_minus = jnp.concatenate([blank_face, middle[..., :-1]], axis=-1)
    slopes = [(x_plus - x_minus) * 0.5, (y_plus - y_minus) * 0.5, (z_plus - z_minus) * 0.5]
    strain = jnp.zeros_like(middle[0])
    for comp_i in range(3):
        for comp_j in range(3):
            sym_part = 0.5 * (slopes[comp_j][comp_i] + slopes[comp_i][comp_j])
            strain = strain + sym_part * sym_part
    viscosity = BASE_VISCOSITY + SMAG_COEF * jnp.sqrt(2.0 * strain)
    laplace = x_plus + x_minus + y_plus + y_minus + z_plus + z_minus - 6.0 * middle
    carried = middle[0:1] * slopes[0] + middle[1:2] * slopes[1] + middle[2:3] * slopes[2]
    return middle + TIME_STEP * (viscosity[None] * laplace - carried + push)


def blade_geometry(frames, substep):
    point_index = jnp.arange(PTS, dtype=jnp.float32)
    radial = RADIUS * (0.2 + 0.8 * (point_index + 0.5) / PTS)
    phases = jnp.arange(3, dtype=jnp.float32) * (2.0 * math.pi / 3.0)
    turning = TIP_SPEED / RADIUS * TIME_STEP * substep
    azimuth = (frames[..., 3:4] + phases + turning)[..., None]
    cosine = jnp.cos(azimuth)
    sine_value = jnp.sin(azimuth)
    x_point = jnp.broadcast_to(frames[..., 0, None, None], frames.shape[:-1] + (3, PTS))
    y_point = frames[..., 1, None, None] + radial * cosine
    z_point = frames[..., 2, None, None] + radial * sine_value
    return (x_point, y_point, z_point, radial, cosine, sine_value)


def choose(onehot, table_row, trailing):
    return jnp.sum(jnp.where(onehot, table_row.reshape((-1,) + (1,) * trailing), 0.0), axis=0)


def blade_forces(
    sampled, radial, cosine, sine_value, bin_table, wear_ids, alive_flags, polar, erosion
):
    section = bin_table[None] == jnp.arange(NSEC, dtype=jnp.int32).reshape(
        (-1,) + (1,) * bin_table.ndim
    )
    lift_base = choose(section, polar[0], bin_table.ndim)
    lift_slope = choose(section, polar[1], bin_table.ndim)
    drag_base = choose(section, polar[2], bin_table.ndim)
    drag_bend = choose(section, polar[3], bin_table.ndim)
    chord_len = choose(section, polar[4], bin_table.ndim)
    wear_state = wear_ids[None] == jnp.arange(NERO, dtype=jnp.int32).reshape(
        (-1,) + (1,) * wear_ids.ndim
    )
    lift_wear = choose(wear_state, erosion[0], wear_ids.ndim)[..., None]
    drag_wear = choose(wear_state, erosion[1], wear_ids.ndim)[..., None]
    normal = sampled[..., 0, :]
    swirl_part = cosine * sampled[..., 2, :] - sine_value * sampled[..., 1, :]
    relative = TIP_SPEED / RADIUS * radial - swirl_part
    speed_mag = jnp.sqrt(normal * normal + relative * relative)
    attack = jnp.arctan2(normal, relative) - TWIST_RATE * (1.0 - radial / RADIUS)
    lift_coef = (lift_base + lift_slope * attack) * lift_wear
    drag_coef = (drag_base + drag_bend * attack * attack) * drag_wear
    half_load = 0.5 * chord_len * speed_mag * alive_flags.astype(jnp.float32)[..., None]
    axial = -half_load * (lift_coef * relative + drag_coef * normal)
    spin_load = -half_load * (lift_coef * normal - drag_coef * relative)
    return jnp.stack([axial, -spin_load * sine_value, spin_load * cosine], axis=-2)


def body(velocity, turbine_frame, turbine_live, polar_bin, erosion_id, polar, erosion):
    brick_x = velocity.shape[1]
    brick_y = velocity.shape[2]
    height = velocity.shape[3]
    frames = with_halo(turbine_frame, (("gx", 0), ("gy", 1)), 1)
    span_x = 6
    span_y = 2 * RADIUS + 6
    span_z = 2 * RADIUS + 6
    anchor = jnp.zeros((), jnp.int32)
    step_whole = jnp.arange(3, dtype=jnp.int32) - 1
    whole_x = jnp.repeat(step_whole * brick_x, 9)
    whole_y = jnp.tile(jnp.repeat(step_whole * brick_y, 3), 3)
    shift_x = whole_x.astype(jnp.float32)
    shift_y = whole_y.astype(jnp.float32)
    hubs = jnp.repeat(frames[..., :3].reshape(9, 3), 3, axis=0)
    depth_start = jnp.clip(jnp.floor(hubs[:, 2]).astype(jnp.int32) - RADIUS - 2, 0, height - span_z)
    spacing = 0.8 * RADIUS / PTS

    def window_start(rel_centre, whole_offset, reach, lowest, count, span):
        raw = jnp.floor(rel_centre).astype(jnp.int32) + whole_offset - reach - lowest + span
        return jnp.clip(raw, 0, count + span)

    def blade_window(blade_item, lowest, count_x, count_y):
        x_row, y_row, z_row, offset_x, offset_y, int_x, int_y, rel_x, rel_y, start_z = blade_item
        start_x = window_start(rel_x, int_x, 2, lowest, count_x, span_x)
        start_y = window_start(rel_y, int_y, RADIUS + 2, lowest, count_y, span_y)
        cells_x = (start_x + lowest - span_x).astype(jnp.float32) + jnp.arange(
            span_x, dtype=jnp.float32
        )
        cells_y = (start_y + lowest - span_y).astype(jnp.float32) + jnp.arange(
            span_y, dtype=jnp.float32
        )
        cells_z = start_z.astype(jnp.float32) + jnp.arange(span_z, dtype=jnp.float32)
        weight_x = kernel((cells_x - offset_x)[:, None] - x_row[None])
        weight_y = kernel((cells_y - offset_y)[:, None] - y_row[None])
        weight_z = kernel(cells_z[:, None] - z_row[None]).astype(jnp.bfloat16)
        return (weight_x[:, None] * weight_y[None], weight_z, (anchor, start_x, start_y, start_z))

    flow_field = velocity
    forces = jnp.zeros((3, 3, PTS), jnp.float32)
    for substep in range(STEPS):
        padded = with_halo(flow_field, (("gx", 1), ("gy", 2)), 1)
        x_point, y_point, z_point, radial, cosine, sine_value = blade_geometry(frames, substep)
        blade_rows = (
            x_point.reshape(27, PTS),
            y_point.reshape(27, PTS),
            z_point.reshape(27, PTS),
            shift_x,
            shift_y,
            whole_x,
            whole_y,
            hubs[:, 0],
            hubs[:, 1],
            depth_start,
        )
        source = jnp.pad(
            flow_field.astype(jnp.bfloat16), ((0, 0), (span_x, span_x), (span_y, span_y), (0, 0))
        )

        def sample_blade(blade_item):
            weight_xy, weight_z, begin = blade_window(blade_item, 0, brick_x, brick_y)
            region = lax.dynamic_slice(source, begin, (3, span_x, span_y, span_z))
            column_sum = jnp.einsum(
                "cxyz,zp->cxyp", region, weight_z, preferred_element_type=jnp.float32
            )
            return jnp.einsum(
                "cxyp,xyp->cp", column_sum, weight_xy, precision=lax.Precision.HIGHEST
            )

        partial_value = lax.map(sample_blade, blade_rows).reshape(3, 3, 3, 3, PTS)
        collected = with_halo(partial_value, (("gx", 0), ("gy", 1)), 1)
        sampled = jnp.sum(collected[::2, ::2], axis=(0, 1))
        loads_forces = blade_forces(
            sampled,
            radial,
            cosine[1, 1],
            sine_value[1, 1],
            polar_bin[0, 0],
            erosion_id[0, 0],
            turbine_live[0, 0],
            polar,
            erosion,
        )
        gathered = with_halo(loads_forces[None, None], (("gx", 0), ("gy", 1)), 1)
        gathered = gathered.reshape(27, 3, PTS)

        def push_blade(grid_push, push_item):
            blade_item, loads = push_item
            weight_xy, weight_z, begin = blade_window(blade_item, 0, brick_x, brick_y)
            weighted = (weight_xy[None] * loads[:, None, None] * spacing).astype(jnp.bfloat16)
            added = jnp.einsum(
                "cxyp,zp->cxyz", weighted, weight_z, preferred_element_type=jnp.float32
            )
            current = lax.dynamic_slice(grid_push, begin, added.shape)
            return (lax.dynamic_update_slice(grid_push, current + added, begin), None)

        start_push = jnp.zeros((3, brick_x + 2 * span_x, brick_y + 2 * span_y, height), jnp.float32)
        grid_push = lax.scan(push_blade, start_push, (blade_rows, gathered))[0]
        forces, grid_push = (
            loads_forces,
            grid_push[:, span_x : span_x + brick_x, span_y : span_y + brick_y],
        )
        flow_field = advance(
            padded[:, 1:-1, 1:-1],
            padded[:, 2:, 1:-1],
            padded[:, :-2, 1:-1],
            padded[:, 1:-1, 2:],
            padded[:, 1:-1, :-2],
            grid_push,
        )
    return (flow_field, (forces / (TIP_SPEED * TIP_SPEED))[None, None])


def solution(mesh):
    return jax.shard_map(
        body,
        mesh=mesh,
        in_specs=(
            P("member", "gx", "gy", None),
            P("gx", "gy", "member"),
            P("gx", "gy", "member"),
            P("gx", "gy", "member", None),
            P("gx", "gy", "member"),
            P(),
            P(),
        ),
        out_specs=(P("member", "gx", "gy", None), P("gx", "gy", "member", None, None)),
        check_vma=False,
    )
```

profile of v0, /device:TPU:0, one launch (start us, length us, event | category | flops | bytes accessed | tf_op | source)
XLA Modules:
  0.0 1774.2 jit_solution(1281859334887195727)
XLA Ops:
  20.4 333.5 %while.56 = (s32[]{:T(128)}, f32[27,3,256]{2,1,0:T(4,128)S(1)}, f32[27]{0:T(128)S(1)}, s32[27]{0:T(128)S(1)}, f32[27]{0:T(128)S(1)}, /*index=5*/f32[27,256]{1,0:...) while((s32[]{:T(128)}, f32[27,3,256]{2,1,0:T(4,128)S(1)}, ...), condition=%wide.region_2.3_spmd, body=%wide.region_1.2_spmd.sunk | while | flops 2612562 | bytes 337175 | solution.py:176
  379.0 525.7 %while.57 = (s32[]{:T(128)}, f32[3,20,56,128]{3,2,1,0:T(8,128)S(1)}, f32[27]{0:T(128)S(1)}, s32[27]{0:T(128)S(1)}, f32[27]{0:T(128)S(1)}, /*index=5*/s32[27]{0:T...) while((s32[]{:T(128)}, ...), condition=%wide.region_11.12_spmd, body=%wide.region_10.11_spmd.sunk | while | flops 2691666 | bytes 334683 | solution.py:204
  392.6 5.8 dynamic_update_slice.44
  412.1 5.8 dynamic_update_slice.44
  431.6 5.8 dynamic_update_slice.44
  451.1 5.8 dynamic_update_slice.44
  470.6 5.8 dynamic_update_slice.44
  490.0 5.8 dynamic_update_slice.44
  567.9 5.8 dynamic_update_slice.44
  587.4 5.8 dynamic_update_slice.44
  606.9 5.8 dynamic_update_slice.44
  626.4 5.8 dynamic_update_slice.44
  645.9 5.8 dynamic_update_slice.44
  665.3 5.8 dynamic_update_slice.44
  743.2 5.8 dynamic_update_slice.44
  762.7 5.8 dynamic_update_slice.44
  782.2 5.8 dynamic_update_slice.44
  801.7 5.8 dynamic_update_slice.44
  821.1 5.8 dynamic_update_slice.44
  840.6 5.8 dynamic_update_slice.44
  906.7 342.3 %while.58 = (s32[]{:T(128)}, f32[27,3,256]{2,1,0:T(4,128)S(1)}, f32[27]{0:T(128)S(1)}, s32[27]{0:T(128)S(1)}, f32[27]{0:T(128)S(1)}, /*index=5*/f32[27,256]{1,0:...) while((s32[]{:T(128)}, f32[27,3,256]{2,1,0:T(4,128)S(1)}, ...), condition=%wide.region_13.14_spmd, body=%wide.region_12.13_spmd.sunk | while | flops 2612562 | bytes 337175 | solution.py:176
  1274.2 499.0 %while.59 = (s32[]{:T(128)}, f32[3,20,56,128]{3,2,1,0:T(8,128)S(1)}, f32[27]{0:T(128)S(1)}, s32[27]{0:T(128)S(1)}, f32[27]{0:T(128)S(1)}, /*index=5*/s32[27]{0:T...) while((s32[]{:T(128)}, ...), condition=%wide.region_16.17_spmd, body=%wide.region_15.16_spmd.sunk | while | flops 2691666 | bytes 334683 | solution.py:204
  1286.9 5.8 dynamic_update_slice.46
  1305.4 5.8 dynamic_update_slice.46
  1323.9 5.8 dynamic_update_slice.46
  1342.4 5.8 dynamic_update_slice.46
  1360.9 5.8 dynamic_update_slice.46
  1379.3 5.8 dynamic_update_slice.46
  1453.3 5.8 dynamic_update_slice.46
  1471.8 5.8 dynamic_update_slice.46
  1490.3 5.8 dynamic_update_slice.46
  1712.1 5.8 dynamic_update_slice.46
  (2108 shorter events, 1049.7 us)
Async XLA Ops:
  0.7 12.5 collective-permute-start.4
  3.8 9.5 collective-permute-start.5
  6.7 12.8 collective-permute-start
  8.6 10.9 collective-permute-start.1
  8.7 359.4 %copy-start.12 = (f32[256]{0:T(256)}, f32[256]{0:T(256)S(1)}, u32[]{:S(2)}) copy-start(f32[256]{0:T(256)S(1)} %get-tuple-element.1295) | copy-start | bytes 3076
  8.7 359.4 %copy-start.14 = (f32[256]{0:T(256)}, f32[256]{0:T(256)S(1)}, u32[]{:S(2)}) copy-start(f32[256]{0:T(256)S(1)} %get-tuple-element.1296) | copy-start | bytes 3076
  13.0 355.1 %copy-start.17 = (f32[3]{0:T(128)}, f32[3]{0:T(128)S(1)}, u32[]{:S(2)}) copy-start(f32[3]{0:T(128)S(1)} %get-tuple-element.1109) | copy-start | bytes 40
  13.0 355.1 %copy-start.19 = (f32[3]{0:T(128)}, f32[3]{0:T(128)S(1)}, u32[]{:S(2)}) copy-start(f32[3]{0:T(128)S(1)} %get-tuple-element.1110) | copy-start | bytes 40
  13.3 1.4 collective-permute-start.7
  13.4 3.0 collective-permute-start.6
  354.0 5.4 collective-permute-start.9
  357.8 5.8 collective-permute-start.8
  363.6 2.4 collective-permute-start.11
  363.7 4.3 collective-permute-start.10
  364.2 6.3 collective-permute-start.3
  365.4 5.1 collective-permute-start.2
  368.4 3.7 collective-permute-start.13
  368.4 5.5 collective-permute-start.12
  374.0 1.7 collective-permute-start.15
  374.1 3.4 collective-permute-start.14
  1249.1 11.5 collective-permute-start.21
  1249.1 11.5 collective-permute-start.20
  1251.1 4.2 collective-permute-start.16
  1253.0 5.8 collective-permute-start.17
  1258.8 3.2 collective-permute-start.19
  1258.9 3.2 collective-permute-start.18
  1260.6 2.4 collective-permute-start.23
  1260.7 3.7 collective-permute-start.22
  1264.8 3.8 collective-permute-start.25
  1264.8 5.5 collective-permute-start.24
  1270.4 1.7 collective-permute-start.27
  1270.5 3.6 collective-permute-start.26
  (44 other events, 2158.2 us)
where the time goes:
time: 1800 us; the launch traced here: 1770 us
  local copies, waits for them, and re-layouts  966 us (54%)
  loops' own time  559 us (31%)
  other arithmetic  163 us (9%)
  waiting for transfers between devices  30.2 us (2%)
  matrix products  28.2 us (2%)
  starting transfers between devices  25.5 us (1%)
    dynamic_slice x972, local copies, waits for them, and re-layouts, body(): partial_value = lax.map(sample_blade, blade_rows).reshape(3, 3, 3, 3, PTS)  625 us
    dynamic_update_slice x54, local copies, waits for them, and re-layouts, push_blade(): return (lax.dynamic_update_slice(grid_push, current + added, begin), None)  314 us
    another operation x2, loops' own time, body(): grid_push = lax.scan(push_blade, start_push, (blade_rows, gathered))[0]  285 us
    another operation x2, loops' own time, body(): partial_value = lax.map(sample_blade, blade_rows).reshape(3, 3, 3, 3, PTS)  275 us
    sub x108, other arithmetic, blade_window(): weight_y = kernel((cells_y - offset_y)[:, None] - y_row[None])  67.8 us
    sub x108, other arithmetic, blade_window(): weight_x = kernel((cells_x - offset_x)[:, None] - x_row[None])  67.8 us
  transfers between devices with their start and end apart: 28, of which 18 were waited for; matrix products, arithmetic and copies ran while one was open for 1% of the time, Pallas kernels for 0%

commit v1 on v0

v1 whole, which is shorter than its diff:
```python
import functools
import math

import jax
import jax.numpy as jnp
from jax import lax
from jax.experimental import pallas as pl
from jax.experimental.pallas import tpu as pltpu
from jax.sharding import PartitionSpec as P

PTS = 256
NSEC = 8
NERO = 16
STEPS = 2
RADIUS = 5
BLADES = 3

TIP_SPEED = 6.0
TIME_STEP = 0.15
BASE_VISCOSITY = 0.1
SMAG_COEF = 0.04
KERNEL_NORM = 35.0 / 96.0
TWIST_RATE = 0.3

MARGIN = 8
DEPTH = 16
LANES = 128
POINTS = BLADES * PTS
SPACING = 0.8 * RADIUS / PTS

OFFSETS = [(ox, oy) for ox in (-1, 0, 1) for oy in (-1, 0, 1)]
OTHERS = [o for o in OFFSETS if o != (0, 0)]
F32 = jnp.float32
BF16 = jnp.bfloat16


def slot(offset):
    return (offset[0] + 1) * 3 + offset[1] + 1


def opposite(offset):
    return (-offset[0], -offset[1])


def phi(distance):
    inside = jnp.maximum(1.0 - distance * distance * (1.0 / 9.0), 0.0)
    return KERNEL_NORM * inside * inside * inside


def halves(value):
    high = value.astype(BF16)
    return high, (value - high.astype(F32)).astype(BF16)


def dot(left, right, left_dim, right_dim):
    return lax.dot_general(
        left, right, (((left_dim,), (right_dim,)), ((), ())), preferred_element_type=F32
    )


def per_blade(rows):
    return jnp.concatenate([rows[b : b + 1] for b in range(BLADES)], axis=1)


def planes_of(ox, brick_x):
    if ox < 0:
        return range(0, 3)
    if ox > 0:
        return range(brick_x - 2, brick_x)
    return range(brick_x)


def rows_of(oy, brick_y):
    if oy < 0:
        return (0, MARGIN)
    if oy > 0:
        return (brick_y - MARGIN, brick_y)
    return (0, brick_y)


def window_rows(oy, brick_y):
    if oy < 0:
        return (brick_y + MARGIN, brick_y + 2 * MARGIN)
    if oy > 0:
        return (0, MARGIN)
    return (MARGIN, MARGIN + brick_y)


def step_kernel(
    count_x,
    count_y,
    u_ref,
    frame_ref,
    live_ref,
    bin_ref,
    wear_ref,
    polar_ref,
    erosion_ref,
    flow_ref,
    load_ref,
    pad_ref,
    yface_ref,
    yhalo_ref,
    fsend_ref,
    frames_ref,
    rsend_ref,
    rows_ref,
    gsend_ref,
    push_ref,
    wx_ref,
    pick_ref,
    wy_ref,
    wz_ref,
    base_ref,
    plane_ref,
    fsem,
    rsem,
    gsem,
    xsem,
    ysem,
):
    brick_x, brick_y, height = u_ref.shape[1:]
    width = brick_y + 2 * MARGIN
    me_x = lax.axis_index("gx")
    me_y = lax.axis_index("gy")

    def neighbour(offset):
        return {
            "gx": lax.rem(me_x + (offset[0] + count_x), count_x),
            "gy": lax.rem(me_y + (offset[1] + count_y), count_y),
        }

    def send(src, dst, sems, target, source_slot, target_slot):
        copy = pltpu.make_async_remote_copy(
            src_ref=src,
            dst_ref=dst,
            send_sem=sems.at[0, source_slot],
            recv_sem=sems.at[1, target_slot],
            device_id=neighbour(target),
            device_id_type=pl.DeviceIdType.MESH,
        )
        copy.start()
        return copy

    barrier = pltpu.get_barrier_semaphore()
    for offset in OTHERS:
        pl.semaphore_signal(
            barrier,
            inc=1,
            device_id=neighbour(offset),
            device_id_type=pl.DeviceIdType.MESH,
        )

    hub_x = frame_ref[0, 0, 0]
    hub_y = frame_ref[0, 0, 1]
    hub_z = frame_ref[0, 0, 2]
    phase = frame_ref[0, 0, 3]
    sub8 = lax.broadcasted_iota(jnp.int32, (8, LANES), 0)
    fsend_ref[...] = jnp.where(sub8 == 0, hub_x, hub_z)
    for comp in range(3):
        yface_ref[0, 0, comp] = u_ref[comp, :, 0, :]
        yface_ref[0, 1, comp] = u_ref[comp, :, brick_y - 1, :]
    pl.semaphore_wait(barrier, len(OTHERS))

    sent = []
    frame_copies = {}
    for offset in OTHERS:
        back = opposite(offset)
        frame_copies[back] = send(
            fsend_ref,
            frames_ref.at[slot(back)],
            fsem,
            offset,
            slot(offset),
            slot(back),
        )
    frames_ref[slot((0, 0))] = fsend_ref[...]

    inner = pl.ds(MARGIN, brick_y)

    def send_faces(substep):
        copies = []
        for side, ox in ((0, -1), (1, 1)):
            plane = 0 if side == 0 else brick_x - 1
            halo = brick_x + 1 if side == 0 else 0
            if substep == 0:
                src = u_ref.at[:, plane]
            else:
                src = pad_ref.at[substep, :, plane + 1, inner]
            copies.append(
                send(
                    src,
                    pad_ref.at[substep, :, halo, inner],
                    xsem.at[substep],
                    (ox, 0),
                    side,
                    side,
                )
            )
        for side, oy in ((0, -1), (1, 1)):
            copies.append(
                send(
                    yface_ref.at[substep, side],
                    yhalo_ref.at[substep, side],
                    ysem.at[substep],
                    (0, oy),
                    side,
                    side,
                )
            )
        return copies

    faces = send_faces(0)
    for comp in range(3):
        for x in range(brick_x):
            pad_ref[0, comp, x + 1, MARGIN : MARGIN + brick_y, :] = u_ref[comp, x]

    lane = lax.broadcasted_iota(jnp.int32, (1, POINTS), 1)
    point = (lane % PTS).astype(F32)
    radial = RADIUS * (0.2 + 0.8 * (point + 0.5) / PTS)
    azimuth = jnp.zeros((8, LANES), F32)
    for substep in range(STEPS):
        for blade in range(BLADES):
            angle = phase + blade * (2.0 * math.pi / 3.0)
            angle = angle + TIP_SPEED / RADIUS * TIME_STEP * substep
            azimuth = jnp.where(sub8 == substep * BLADES + blade, angle, azimuth)
    cosines = jnp.cos(azimuth)
    sines = jnp.sin(azimuth)

    def trig_row(table, substep):
        rows = [table[substep * BLADES + b : substep * BLADES + b + 1] for b in range(BLADES)]
        return jnp.concatenate([r for r in rows for _ in range(PTS // LANES)], axis=1)

    cos_rows = [trig_row(cosines, s) for s in range(STEPS)]
    sin_rows = [trig_row(sines, s) for s in range(STEPS)]
    depth_start = jnp.clip(
        jnp.floor(jnp.full((1, LANES), hub_z, F32)) - (RADIUS + 2), 0.0, height - DEPTH
    )[:, 0:1]

    def point_weights(substep):
        y_point = hub_y + radial * cos_rows[substep]
        z_point = hub_z + radial * sin_rows[substep]
        cells_y = lax.broadcasted_iota(jnp.int32, (width, 1), 0).astype(F32) - MARGIN
        wy_ref[substep] = phi(cells_y - y_point)
        cells_z = depth_start + lax.broadcasted_iota(jnp.int32, (DEPTH, 1), 0).astype(F32)
        wz_ref[substep] = phi(cells_z - z_point).astype(BF16)

    for substep in range(STEPS):
        point_weights(substep)

    bins = bin_ref[0, 0]
    tables = []
    for row in range(5):
        table = jnp.zeros((BLADES, PTS), F32)
        for entry in range(NSEC):
            table = jnp.where(bins == entry, polar_ref[row, entry], table)
        tables.append(per_blade(table))
    lift_base, lift_slope, drag_base, drag_bend, chord = tables

    def wear_row(row):
        parts = [
            jnp.full((1, PTS), erosion_ref[row, wear_ref[0, 0, b]], F32) for b in range(BLADES)
        ]
        return jnp.concatenate(parts, axis=1)

    lift_wear = wear_row(0)
    drag_wear = wear_row(1)
    live = live_ref[0, 0, 0].astype(F32)

    x_index = lax.broadcasted_iota(jnp.int32, (brick_x, LANES), 0).astype(F32)
    z_index = lax.broadcasted_iota(jnp.int32, (DEPTH, height), 1).astype(F32)
    k_index = lax.broadcasted_iota(jnp.int32, (DEPTH, height), 0).astype(F32)

    def prepare(offset):
        t = slot(offset)
        wx_ref[t] = phi(x_index - float(offset[0] * brick_x) - frames_ref[t, 0:1, :])
        start = jnp.clip(
            jnp.floor(frames_ref[t, 1:2, :]) - (RADIUS + 2), 0.0, float(height - DEPTH)
        )
        pick_ref[t] = jnp.where(z_index - start == k_index, 1.0, 0.0).astype(BF16)

    def load_half(substep, comp, x, rows):
        cells = pad_ref[substep, comp, x + 1, MARGIN + rows[0] : MARGIN + rows[1], :]
        return cells.astype(BF16).astype(F32)

    def contracted(substep, offset):
        t = slot(offset)
        rows = rows_of(offset[1], brick_y)
        place = window_rows(offset[1], brick_y)
        parts = []
        for comp in range(3):
            total = None
            for x in planes_of(offset[0], brick_x):
                term = wx_ref[t, x : x + 1, :] * load_half(substep, comp, x, rows)
                total = term if total is None else total + term
            if place[0]:
                parts.append(jnp.zeros((place[0], height), F32))
            parts.append(total)
            if width - place[1]:
                parts.append(jnp.zeros((width - place[1], height), F32))
        parts.append(jnp.zeros((LANES - 3 * width, height), F32))
        high, low = halves(jnp.concatenate(parts, axis=0))
        pick = pick_ref[t]
        return dot(pick, high, 1, 1) + dot(pick, low, 1, 1)

    z_lane = lax.broadcasted_iota(jnp.int32, (8, height), 1)

    def stencil(substep, begin, end):
        def one(x, carry):
            for y in range(0, brick_y, 8):
                row = MARGIN + y
                mid, diff, lap = [], [], []
                for c in range(3):
                    m = pad_ref[substep, c, x + 1, row : row + 8, :]
                    xp = pad_ref[substep, c, x + 2, row : row + 8, :]
                    xm = pad_ref[substep, c, x, row : row + 8, :]
                    yp = pad_ref[substep, c, x + 1, row + 1 : row + 9, :]
                    ym = pad_ref[substep, c, x + 1, row - 1 : row + 7, :]
                    zp = jnp.where(z_lane == height - 1, 0.0, pltpu.roll(m, height - 1, 1))
                    zm = jnp.where(z_lane == 0, 0.0, pltpu.roll(m, 1, 1))
                    mid.append(m)
                    diff.append((xp - xm, yp - ym, zp - zm))
                    lap.append(((xp + xm) + (yp + ym)) + ((zp + zm) - 6.0 * m))
                cross = [diff[i][j] + diff[j][i] for i, j in ((0, 1), (0, 2), (1, 2))]
                straight = sum(diff[i][i] * diff[i][i] for i in range(3))
                strain2 = 0.5 * straight + 0.25 * sum(v * v for v in cross)
                visc = BASE_VISCOSITY + SMAG_COEF * jnp.sqrt(strain2)
                for c in range(3):
                    carried = sum(mid[j] * diff[c][j] for j in range(3))
                    base_ref[c, x, y : y + 8, :] = mid[c] + TIME_STEP * (
                        visc * lap[c] - 0.5 * carried
                    )
            return carry

        lax.fori_loop(begin, end, one, 0)

    def place_y_halo(substep):
        for comp in range(3):
            pad_ref[substep, comp, 1 : brick_x + 1, MARGIN + brick_y, :] = yhalo_ref[
                substep, 0, comp
            ]
            pad_ref[substep, comp, 1 : brick_x + 1, MARGIN - 1, :] = yhalo_ref[substep, 1, comp]

    prepare((0, 0))
    for substep in range(STEPS):
        row_copies = {}
        for offset in OTHERS:
            if substep == 0:
                frame_copies[offset].wait_recv()
                prepare(offset)
            t = slot(offset)
            rsend_ref[substep, t] = contracted(substep, offset)
            back = opposite(offset)
            row_copies[back] = send(
                rsend_ref.at[substep, t],
                rows_ref.at[substep, slot(back)],
                rsem.at[substep],
                offset,
                t,
                slot(back),
            )
        if substep > 0:
            faces = send_faces(substep)
        window = contracted(substep, (0, 0))
        for copy in faces:
            copy.wait_recv()
        sent += faces
        place_y_halo(substep)
        stencil(substep, 0, brick_x // 2)

        for offset in OTHERS:
            row_copies[offset].wait_recv()
            window = window + rows_ref[substep, slot(offset)]
        sent += list(row_copies.values())
        high, low = halves(window)
        wz = wz_ref[substep]
        column = dot(high, wz, 0, 0) + dot(low, wz, 0, 0)
        wy = wy_ref[substep]
        velocity = [
            jnp.sum(column[c * width : (c + 1) * width] * wy, axis=0, keepdims=True)
            for c in range(3)
        ]

        cosine, sine = cos_rows[substep], sin_rows[substep]
        normal = velocity[0]
        relative = TIP_SPEED / RADIUS * radial - (cosine * velocity[2] - sine * velocity[1])
        speed = jnp.sqrt(normal * normal + relative * relative)
        attack = jnp.arctan2(normal, relative) - TWIST_RATE * (1.0 - radial / RADIUS)
        lift = (lift_base + lift_slope * attack) * lift_wear
        drag = (drag_base + drag_bend * attack * attack) * drag_wear
        half_load = 0.5 * chord * speed * live
        axial = -half_load * (lift * relative + drag * normal)
        spin = -half_load * (lift * normal - drag * relative)
        force = [axial, -spin * sine, spin * cosine]

        spread = [(wy * (force[c] * SPACING)).astype(BF16) for c in range(3)]
        spread.append(jnp.zeros((LANES - 3 * width, POINTS), BF16))
        gsend_ref[substep] = dot(wz, jnp.concatenate(spread, axis=0), 1, 1)
        push_copies = {}
        for offset in OTHERS:
            back = opposite(offset)
            push_copies[back] = send(
                gsend_ref.at[substep],
                push_ref.at[substep, slot(back)],
                gsem.at[substep],
                offset,
                slot(offset),
                slot(back),
            )
        if substep == STEPS - 1:
            for c in range(3):
                scaled = force[c] * (1.0 / (TIP_SPEED * TIP_SPEED))
                for b in range(BLADES):
                    load_ref[0, 0, b, c : c + 1, :] = scaled[:, b * PTS : (b + 1) * PTS]
        stencil(substep, brick_x // 2, brick_x)

        def expand(offset, part):
            t = slot(offset)
            high, low = halves(part)
            pick = pick_ref[t]
            plane_ref[t] = dot(high, pick, 0, 0) + dot(low, pick, 0, 0)

        expand((0, 0), gsend_ref[substep])
        for offset in OTHERS:
            push_copies[offset].wait_recv()
            expand(offset, push_ref[substep, slot(offset)])
        sent += list(push_copies.values())

        for c in range(3):
            for y in range(0, brick_y, 8):
                for x in range(brick_x):
                    total = None
                    for offset in OFFSETS:
                        rows = rows_of(offset[1], brick_y)
                        if x not in planes_of(offset[0], brick_x):
                            continue
                        if not rows[0] <= y < rows[1]:
                            continue
                        t = slot(offset)
                        row = c * width + window_rows(offset[1], brick_y)[0] + y - rows[0]
                        term = wx_ref[t, x : x + 1, :] * plane_ref[t, row : row + 8, :]
                        total = term if total is None else total + term
                    new = base_ref[c, x, y : y + 8, :] + TIME_STEP * total
                    if substep == STEPS - 1:
                        flow_ref[c, x, y : y + 8, :] = new
                    else:
                        row = MARGIN + y
                        pad_ref[substep + 1, c, x + 1, row : row + 8, :] = new
                        if y == 0:
                            yface_ref[substep + 1, 0, c, x : x + 1, :] = new[0:1]
                        if y == brick_y - 8:
                            yface_ref[substep + 1, 1, c, x : x + 1, :] = new[7:8]

    for copy in list(frame_copies.values()) + sent:
        copy.wait_send()


def body(velocity, turbine_frame, turbine_live, polar_bin, erosion_id, polar, erosion):
    comps, brick_x, brick_y, height = velocity.shape
    width = brick_y + 2 * MARGIN
    vmem = pl.BlockSpec(memory_space=pltpu.VMEM)
    smem = pl.BlockSpec(memory_space=pltpu.SMEM)
    turbines = len(OFFSETS)
    return pl.pallas_call(
        functools.partial(step_kernel, lax.axis_size("gx"), lax.axis_size("gy")),
        out_shape=(
            jax.ShapeDtypeStruct(velocity.shape, F32),
            jax.ShapeDtypeStruct((1, 1, BLADES, 3, PTS), F32),
        ),
        in_specs=[vmem, smem, smem, vmem, smem, smem, smem],
        out_specs=(vmem, vmem),
        scratch_shapes=[
            pltpu.VMEM((STEPS, comps, brick_x + 2, width, height), F32),
            pltpu.VMEM((STEPS, 2, comps, brick_x, height), F32),
            pltpu.VMEM((STEPS, 2, comps, brick_x, height), F32),
            pltpu.VMEM((8, LANES), F32),
            pltpu.VMEM((turbines, 8, LANES), F32),
            pltpu.VMEM((STEPS, turbines, DEPTH, LANES), F32),
            pltpu.VMEM((STEPS, turbines, DEPTH, LANES), F32),
            pltpu.VMEM((STEPS, DEPTH, LANES), F32),
            pltpu.VMEM((STEPS, turbines, DEPTH, LANES), F32),
            pltpu.VMEM((turbines, brick_x, LANES), F32),
            pltpu.VMEM((turbines, DEPTH, height), BF16),
            pltpu.VMEM((STEPS, width, POINTS), F32),
            pltpu.VMEM((STEPS, DEPTH, POINTS), BF16),
            pltpu.VMEM((comps, brick_x, brick_y, height), F32),
            pltpu.VMEM((turbines, LANES, height), F32),
            pltpu.SemaphoreType.DMA((2, turbines)),
            pltpu.SemaphoreType.DMA((STEPS, 2, turbines)),
            pltpu.SemaphoreType.DMA((STEPS, 2, turbines)),
            pltpu.SemaphoreType.DMA((STEPS, 2, 2)),
            pltpu.SemaphoreType.DMA((STEPS, 2, 2)),
        ],
        compiler_params=pltpu.CompilerParams(
            collective_id=0, has_side_effects=True, vmem_limit_bytes=32 * 1024 * 1024
        ),
    )(velocity, turbine_frame, turbine_live, polar_bin, erosion_id, polar, erosion)


def solution(mesh):
    return jax.shard_map(
        body,
        mesh=mesh,
        in_specs=(
            P("member", "gx", "gy", None),
            P("gx", "gy", "member"),
            P("gx", "gy", "member"),
            P("gx", "gy", "member", None),
            P("gx", "gy", "member"),
            P(),
            P(),
        ),
        out_specs=(P("member", "gx", "gy", None), P("gx", "gy", "member", None, None)),
        check_vma=False,
    )
```

time: 1800 us -> 37 us (0.02); the launches traced: 1770 us -> 36.8 us
  local copies, waits for them, and re-layouts: 966 us -> 3 us
  loops' own time: 559 us -> 0 us
  other arithmetic: 163 us -> 0 us
  Pallas kernels: 0 us -> 32.5 us
  waiting for transfers between devices: 30.2 us -> 0 us
  matrix products: 28.2 us -> 0 us
  starting transfers between devices: 25.5 us -> 0 us
    dynamic_slice x972 -> x0, local copies, waits for them, and re-layouts: 625 us -> none  [body(): partial_value = lax.map(sample_blade, blade_rows).reshape(3, 3, 3, 3, PTS)]
    another operation x4 -> x0, loops' own time: 559 us -> none  [the longest x2 285 us: body(): grid_push = lax.scan(push_blade, start_push, (blade_rows, gathered))[0]]
    dynamic_update_slice x108 -> x0, local copies, waits for them, and re-layouts: 315 us -> none  [the longest x54 314 us: push_blade(): return (lax.dynamic_update_slice(grid_push, current + added, begin), None)]
    sub x216 -> x0, other arithmetic: 136 us -> none  [the longest x108 67.8 us: blade_window(): weight_y = kernel((cells_y - offset_y)[:, None] - y_row[None])]
    pallas_call x0 -> x1, Pallas kernels: none -> 32.5 us  [body(): pl.pallas_call(functools.partial(step_kernel, lax.axis_size('gx'), lax.ax...]
    ppermute x28 -> x0, waiting for transfers between devices: 30.2 us -> none  [the longest x14 20.8 us: with_halo(): lax.ppermute(tail, axis, [(i, (i + 1) % count) for i in range(count)])]
    dot_general x108 -> x0, matrix products: 28.2 us -> none  [the longest x54 15 us: sample_blade(): jnp.einsum('cxyz,zp->cxyp', region, weight_z, preferred_element_type=jnp....]
    ppermute x28 -> x0, starting transfers between devices: 25.5 us -> none  [the longest x14 13 us: with_halo(): lax.ppermute(tail, axis, [(i, (i + 1) % count) for i in range(count)])]
  transfers between devices with their start and end apart: 28 -> 0, of which waited for: 18 -> 0; matrix products, arithmetic and copies ran while one was open for 1% -> 0% of each run, Pallas kernels for 0% -> 0%
where the time goes in v1:
time: 37 us; the launch traced here: 36.8 us
  Pallas kernels  32.5 us (88%)
  local copies, waits for them, and re-layouts  3 us (8%)
  between operations  1.35 us (4%)
    pallas_call x1, Pallas kernels, body(): pl.pallas_call(functools.partial(step_kernel, lax.axis_size('gx'), lax.ax...  32.5 us
    unnamed x12, local copies, waits for them, and re-layouts  2.39 us

profile of v1, /device:TPU:0, one launch (start us, length us, event | category | flops | bytes accessed | tf_op | source)
XLA Modules:
  0.0 36.8 jit_solution(13692610717957175586)
XLA Ops:
  0.6 0.0 copy-start.1
  1.3 0.0 copy-start.2
  1.3 0.0 copy-start.3
  1.3 0.0 copy-start.4
  1.3 0.7 %copy.9.bin_ref = s32[1,1,3,256]{3,2,1,0:T(4,128)S(1)} copy(s32[1,1,3,256]{3,1,2,0:T(1,128)} %param.10) | data formatting | bytes 6144 | tf_op args[3]
  2.0 0.0 copy-done.1
  2.0 0.0 copy-done.2
  2.0 0.0 copy-done.3
  2.0 0.0 copy-done.4
  2.1 0.0 copy-start
  2.1 1.0 %copy-done = f32[3,8,24,128]{3,2,1,0:T(8,128)S(1)} copy-done((f32[3,8,24,128]{3,2,1,0:T(8,128)S(1)}, f32[3,8,24,128]{3,2,1,0:T(8,128)}, u32[]{:S(2)}) %copy-start) | copy-done | bytes 294936
  3.0 32.5 %shard_map.86 = (f32[3,8,24,128]{3,2,1,0:T(8,128)S(1)}, f32[1,1,3,3,256]{4,3,2,1,0:T(4,128)S(1)}) custom-call(f32[3,8,24,128]{3,2,1,0:T(8,128)S(1)} %copy-done, f32[1,1,4]{2,1,0:T(1,128)S(1)} %copy-done.3, s32[1,1,1]{2,1,0:T(1,128)S(6)} %copy.12.live_ref, s32[1,1,3,256]{3,2,1,0:T(4,128)S(1)} %copy.9.bin_ref, s32[1,1,3]{2,1,0:T(1,128)S(1)} %copy-done.4, ...), custom_call_target="tpu_custom_call" | custom-call | tf_op jit(solution)/shard_map/pallas_call | solution.py:464
  35.5 0.6 %copy.10 = f32[1,1,3,3,256]{4,1,3,2,0:T(1,128)} copy(f32[1,1,3,3,256]{4,3,2,1,0:T(4,128)S(1)} %get-tuple-element.3) | data formatting | bytes 18432 | tf_op jit(solution)/shard_map/pallas_call | solution.py:464
  36.1 0.7 %copy.13 = f32[3,8,24,128]{3,2,1,0:T(8,128)} copy(f32[3,8,24,128]{3,2,1,0:T(8,128)S(1)} %get-tuple-element.6) | data formatting | bytes 589824
Async XLA Ops:
  0.6 1.4 %copy-start.1 = (f32[5,8]{1,0:T(8,128)S(1)}, f32[5,8]{1,0:T(8,128)}, u32[]{:S(2)}) copy-start(f32[5,8]{1,0:T(8,128)} %polar_ref.1) | copy-start | bytes 484
  1.3 0.7 %copy-start.2 = (f32[2,16]{1,0:T(2,128)S(1)}, f32[2,16]{1,0:T(2,128)}, u32[]{:S(2)}) copy-start(f32[2,16]{1,0:T(2,128)} %erosion_ref.1) | copy-start | bytes 388
  1.3 0.7 %copy-start.3 = (f32[1,1,4]{2,1,0:T(1,128)S(1)}, f32[1,1,4]{2,1,0:T(1,128)}, u32[]{:S(2)}) copy-start(f32[1,1,4]{2,1,0:T(1,128)} %frame_ref.1) | copy-start | bytes 52
  1.3 0.7 %copy-start.4 = (s32[1,1,3]{2,1,0:T(1,128)S(1)}, s32[1,1,3]{2,1,0:T(1,128)}, u32[]{:S(2)}) copy-start(s32[1,1,3]{2,1,0:T(1,128)} %wear_ref.1) | copy-start | bytes 40
  2.1 1.0 %copy-start = (f32[3,8,24,128]{3,2,1,0:T(8,128)S(1)}, f32[3,8,24,128]{3,2,1,0:T(8,128)}, u32[]{:S(2)}) copy-start(f32[3,8,24,128]{3,2,1,0:T(8,128)} %u_ref.1) | copy-start | bytes 884740

commit v2 on v1

--- a/solution.py
+++ b/solution.py
@@ -29,7 +29,9 @@
 SPACING = 0.8 * RADIUS / PTS
 
 OFFSETS = [(ox, oy) for ox in (-1, 0, 1) for oy in (-1, 0, 1)]
-OTHERS = [o for o in OFFSETS if o != (0, 0)]
+ACROSS = [(-1, 0), (1, 0), (-1, -1), (-1, 1), (1, -1), (1, 1)]
+BESIDE = [(0, -1), (0, 1)]
+OTHERS = ACROSS + BESIDE
 F32 = jnp.float32
 BF16 = jnp.bfloat16
 
@@ -89,13 +91,13 @@
 def step_kernel(
     count_x,
     count_y,
-    u_ref,
-    frame_ref,
-    live_ref,
-    bin_ref,
-    wear_ref,
-    polar_ref,
-    erosion_ref,
+    u_hbm,
+    frame_hbm,
+    live_hbm,
+    bin_hbm,
+    wear_hbm,
+    polar_hbm,
+    erosion_hbm,
     flow_ref,
     load_ref,
     pad_ref,
@@ -113,13 +115,20 @@
     wz_ref,
     base_ref,
     plane_ref,
+    frame_ref,
+    live_ref,
+    bin_ref,
+    wear_ref,
+    polar_ref,
+    erosion_ref,
+    load_sem,
     fsem,
     rsem,
     gsem,
     xsem,
     ysem,
 ):
-    brick_x, brick_y, height = u_ref.shape[1:]
+    brick_x, brick_y, height = u_hbm.shape[1:]
     width = brick_y + 2 * MARGIN
     me_x = lax.axis_index("gx")
     me_y = lax.axis_index("gy")
@@ -151,15 +160,29 @@
             device_id_type=pl.DeviceIdType.MESH,
         )
 
+    inner = pl.ds(MARGIN, brick_y)
+    fetches = []
+    for n, (src, dst) in enumerate(
+        (
+            (frame_hbm, frame_ref),
+            (u_hbm, pad_ref.at[0, :, pl.ds(1, brick_x), inner]),
+            (live_hbm, live_ref),
+            (bin_hbm, bin_ref),
+            (wear_hbm, wear_ref),
+            (polar_hbm, polar_ref),
+            (erosion_hbm, erosion_ref),
+        )
+    ):
+        fetch = pltpu.make_async_copy(src, dst, load_sem.at[n])
+        fetch.start()
+        fetches.append(fetch)
+    fetches[0].wait()
     hub_x = frame_ref[0, 0, 0]
     hub_y = frame_ref[0, 0, 1]
     hub_z = frame_ref[0, 0, 2]
     phase = frame_ref[0, 0, 3]
     sub8 = lax.broadcasted_iota(jnp.int32, (8, LANES), 0)
     fsend_ref[...] = jnp.where(sub8 == 0, hub_x, hub_z)
-    for comp in range(3):
-        yface_ref[0, 0, comp] = u_ref[comp, :, 0, :]
-        yface_ref[0, 1, comp] = u_ref[comp, :, brick_y - 1, :]
     pl.semaphore_wait(barrier, len(OTHERS))
 
     sent = []
@@ -176,20 +199,14 @@
         )
     frames_ref[slot((0, 0))] = fsend_ref[...]
 
-    inner = pl.ds(MARGIN, brick_y)
-
     def send_faces(substep):
         copies = []
         for side, ox in ((0, -1), (1, 1)):
             plane = 0 if side == 0 else brick_x - 1
             halo = brick_x + 1 if side == 0 else 0
-            if substep == 0:
-                src = u_ref.at[:, plane]
-            else:
-                src = pad_ref.at[substep, :, plane + 1, inner]
             copies.append(
                 send(
-                    src,
+                    pad_ref.at[substep, :, plane + 1, inner],
                     pad_ref.at[substep, :, halo, inner],
                     xsem.at[substep],
                     (ox, 0),
@@ -210,10 +227,12 @@
             )
         return copies
 
+    for fetch in fetches[1:]:
+        fetch.wait()
+    for comp in range(3):
+        yface_ref[0, 0, comp] = pad_ref[0, comp, 1 : brick_x + 1, MARGIN, :]
+        yface_ref[0, 1, comp] = pad_ref[0, comp, 1 : brick_x + 1, MARGIN + brick_y - 1, :]
     faces = send_faces(0)
-    for comp in range(3):
-        for x in range(brick_x):
-            pad_ref[0, comp, x + 1, MARGIN : MARGIN + brick_y, :] = u_ref[comp, x]
 
     lane = lax.broadcasted_iota(jnp.int32, (1, POINTS), 1)
     point = (lane % PTS).astype(F32)
@@ -245,10 +264,9 @@
         cells_z = depth_start + lax.broadcasted_iota(jnp.int32, (DEPTH, 1), 0).astype(F32)
         wz_ref[substep] = phi(cells_z - z_point).astype(BF16)
 
-    for substep in range(STEPS):
-        point_weights(substep)
-
-    bins = bin_ref[0, 0]
+    point_weights(0)
+
+    bins = jnp.concatenate([bin_ref[0, b] for b in range(BLADES)], axis=0)
     tables = []
     for row in range(5):
         table = jnp.zeros((BLADES, PTS), F32)
@@ -277,7 +295,8 @@
         start = jnp.clip(
             jnp.floor(frames_ref[t, 1:2, :]) - (RADIUS + 2), 0.0, float(height - DEPTH)
         )
-        pick_ref[t] = jnp.where(z_index - start == k_index, 1.0, 0.0).astype(BF16)
+        pick = jnp.where(z_index - start == k_index, 1.0, 0.0).astype(BF16)
+        pick_ref[t] = jnp.concatenate([pick, pick], axis=0)
 
     def load_half(substep, comp, x, rows):
         cells = pad_ref[substep, comp, x + 1, MARGIN + rows[0] : MARGIN + rows[1], :]
@@ -300,8 +319,10 @@
                 parts.append(jnp.zeros((width - place[1], height), F32))
         parts.append(jnp.zeros((LANES - 3 * width, height), F32))
         high, low = halves(jnp.concatenate(parts, axis=0))
-        pick = pick_ref[t]
-        return dot(pick, high, 1, 1) + dot(pick, low, 1, 1)
+        pick = pick_ref[t, 0:DEPTH, :]
+        return dot(
+            jnp.concatenate([pick, pick], axis=1), jnp.concatenate([high, low], axis=1), 1, 1
+        )
 
     z_lane = lax.broadcasted_iota(jnp.int32, (8, height), 1)
 
@@ -341,34 +362,87 @@
             ]
             pad_ref[substep, comp, 1 : brick_x + 1, MARGIN - 1, :] = yhalo_ref[substep, 1, comp]
 
+    def send_rows(substep, offsets):
+        parts = [contracted(substep, offset) for offset in offsets]
+        for offset, part in zip(offsets, parts):
+            rsend_ref[substep, slot(offset)] = part
+        copies = {}
+        for offset in offsets:
+            back = opposite(offset)
+            copies[back] = send(
+                rsend_ref.at[substep, slot(offset)],
+                rows_ref.at[substep, slot(back)],
+                rsem.at[substep],
+                offset,
+                slot(offset),
+                slot(back),
+            )
+        return copies
+
+    def finish(substep, c, x, y, new):
+        if substep == STEPS - 1:
+            flow_ref[c, x, y : y + 8, :] = new
+        else:
+            row = MARGIN + y
+            pad_ref[substep + 1, c, x + 1, row : row + 8, :] = new
+            if y == 0:
+                yface_ref[substep + 1, 0, c, x : x + 1, :] = new[0:1]
+            if y == brick_y - 8:
+                yface_ref[substep + 1, 1, c, x : x + 1, :] = new[7:8]
+
+    edges = sorted(set(planes_of(-1, brick_x)) | set(planes_of(1, brick_x)))
+
+    def add_push(substep, offsets, planes, last):
+        for c in range(3):
+            for y in range(0, brick_y, 8):
+                for x in planes:
+                    total = None
+                    for offset in offsets:
+                        rows = rows_of(offset[1], brick_y)
+                        if x not in planes_of(offset[0], brick_x):
+                            continue
+                        if not rows[0] <= y < rows[1]:
+                            continue
+                        t = slot(offset)
+                        row = c * width + window_rows(offset[1], brick_y)[0] + y - rows[0]
+                        term = wx_ref[t, x : x + 1, :] * plane_ref[t, row : row + 8, :]
+                        total = term if total is None else total + term
+                    new = base_ref[c, x, y : y + 8, :] + TIME_STEP * total
+                    if last or x not in edges:
+                        finish(substep, c, x, y, new)
+                    else:
+                        base_ref[c, x, y : y + 8, :] = new
+
     prepare((0, 0))
     for substep in range(STEPS):
         row_copies = {}
-        for offset in OTHERS:
-            if substep == 0:
+        if substep == 0:
+            for offset in BESIDE:
                 frame_copies[offset].wait_recv()
                 prepare(offset)
-            t = slot(offset)
-            rsend_ref[substep, t] = contracted(substep, offset)
-            back = opposite(offset)
-            row_copies[back] = send(
-                rsend_ref.at[substep, t],
-                rows_ref.at[substep, slot(back)],
-                rsem.at[substep],
-                offset,
-                t,
-                slot(back),
-            )
-        if substep > 0:
+            row_copies.update(send_rows(substep, BESIDE))
+            window = contracted(substep, (0, 0))
+            for offset in ACROSS:
+                frame_copies[offset].wait_recv()
+                prepare(offset)
+            row_copies.update(send_rows(substep, ACROSS))
+        else:
+            row_copies.update(send_rows(substep, ACROSS))
+            row_copies.update(send_rows(substep, BESIDE))
             faces = send_faces(substep)
-        window = contracted(substep, (0, 0))
-        for copy in faces:
+            window = contracted(substep, (0, 0))
+        sent += faces
+        for copy in faces[2:]:
             copy.wait_recv()
-        sent += faces
         place_y_halo(substep)
-        stencil(substep, 0, brick_x // 2)
-
-        for offset in OTHERS:
+        if substep == 0:
+            for copy in faces[:2]:
+                copy.wait_recv()
+            stencil(substep, 0, brick_x)
+        else:
+            stencil(substep, 1, brick_x - 1)
+
+        for offset in BESIDE + ACROSS:
             row_copies[offset].wait_recv()
             window = window + rows_ref[substep, slot(offset)]
         sent += list(row_copies.values())
@@ -411,45 +485,31 @@
             for c in range(3):
                 scaled = force[c] * (1.0 / (TIP_SPEED * TIP_SPEED))
                 for b in range(BLADES):
-                    load_ref[0, 0, b, c : c + 1, :] = scaled[:, b * PTS : (b + 1) * PTS]
-        stencil(substep, brick_x // 2, brick_x)
+                    load_ref[0, b, c] = scaled[:, b * PTS : (b + 1) * PTS]
+        if substep + 1 < STEPS:
+            point_weights(substep + 1)
+        if substep > 0:
+            for copy in faces[:2]:
+                copy.wait_recv()
+            stencil(substep, 0, 1)
+            stencil(substep, brick_x - 1, brick_x)
 
         def expand(offset, part):
             t = slot(offset)
             high, low = halves(part)
-            pick = pick_ref[t]
-            plane_ref[t] = dot(high, pick, 0, 0) + dot(low, pick, 0, 0)
+            plane_ref[t] = dot(jnp.concatenate([high, low], axis=0), pick_ref[t], 0, 0)
 
         expand((0, 0), gsend_ref[substep])
-        for offset in OTHERS:
+        for offset in BESIDE:
             push_copies[offset].wait_recv()
             expand(offset, push_ref[substep, slot(offset)])
+        add_push(substep, [(0, 0)] + BESIDE, range(brick_x), False)
+        for offset in ACROSS:
+            push_copies[offset].wait_recv()
+        for offset in ACROSS:
+            expand(offset, push_ref[substep, slot(offset)])
+        add_push(substep, ACROSS, edges, True)
         sent += list(push_copies.values())
-
-        for c in range(3):
-            for y in range(0, brick_y, 8):
-                for x in range(brick_x):
-                    total = None
-                    for offset in OFFSETS:
-                        rows = rows_of(offset[1], brick_y)
-                        if x not in planes_of(offset[0], brick_x):
-                            continue
-                        if not rows[0] <= y < rows[1]:
-                            continue
-                        t = slot(offset)
-                        row = c * width + window_rows(offset[1], brick_y)[0] + y - rows[0]
-                        term = wx_ref[t, x : x + 1, :] * plane_ref[t, row : row + 8, :]
-                        total = term if total is None else total + term
-                    new = base_ref[c, x, y : y + 8, :] + TIME_STEP * total
-                    if substep == STEPS - 1:
-                        flow_ref[c, x, y : y + 8, :] = new
-                    else:
-                        row = MARGIN + y
-                        pad_ref[substep + 1, c, x + 1, row : row + 8, :] = new
-                        if y == 0:
-                            yface_ref[substep + 1, 0, c, x : x + 1, :] = new[0:1]
-                        if y == brick_y - 8:
-                            yface_ref[substep + 1, 1, c, x : x + 1, :] = new[7:8]
 
     for copy in list(frame_copies.values()) + sent:
         copy.wait_send()
@@ -459,15 +519,14 @@
     comps, brick_x, brick_y, height = velocity.shape
     width = brick_y + 2 * MARGIN
     vmem = pl.BlockSpec(memory_space=pltpu.VMEM)
-    smem = pl.BlockSpec(memory_space=pltpu.SMEM)
     turbines = len(OFFSETS)
-    return pl.pallas_call(
+    flow, load = pl.pallas_call(
         functools.partial(step_kernel, lax.axis_size("gx"), lax.axis_size("gy")),
         out_shape=(
             jax.ShapeDtypeStruct(velocity.shape, F32),
-            jax.ShapeDtypeStruct((1, 1, BLADES, 3, PTS), F32),
+            jax.ShapeDtypeStruct((1, BLADES, 3, 1, PTS), F32),
         ),
-        in_specs=[vmem, smem, smem, vmem, smem, smem, smem],
+        in_specs=[pl.BlockSpec(memory_space=pltpu.HBM)] * 7,
         out_specs=(vmem, vmem),
         scratch_shapes=[
             pltpu.VMEM((STEPS, comps, brick_x + 2, width, height), F32),
@@ -480,11 +539,18 @@
             pltpu.VMEM((STEPS, DEPTH, LANES), F32),
             pltpu.VMEM((STEPS, turbines, DEPTH, LANES), F32),
             pltpu.VMEM((turbines, brick_x, LANES), F32),
-            pltpu.VMEM((turbines, DEPTH, height), BF16),
+            pltpu.VMEM((turbines, 2 * DEPTH, height), BF16),
             pltpu.VMEM((STEPS, width, POINTS), F32),
             pltpu.VMEM((STEPS, DEPTH, POINTS), BF16),
             pltpu.VMEM((comps, brick_x, brick_y, height), F32),
             pltpu.VMEM((turbines, LANES, height), F32),
+            pltpu.SMEM(turbine_frame.shape, F32),
+            pltpu.SMEM(turbine_live.shape, jnp.int32),
+            pltpu.VMEM((1, BLADES, 1, PTS), jnp.int32),
+            pltpu.SMEM(erosion_id.shape, jnp.int32),
+            pltpu.SMEM(polar.shape, F32),
+            pltpu.SMEM(erosion.shape, F32),
+            pltpu.SemaphoreType.DMA((7,)),
             pltpu.SemaphoreType.DMA((2, turbines)),
             pltpu.SemaphoreType.DMA((STEPS, 2, turbines)),
             pltpu.SemaphoreType.DMA((STEPS, 2, turbines)),
@@ -492,9 +558,18 @@
             pltpu.SemaphoreType.DMA((STEPS, 2, 2)),
         ],
         compiler_params=pltpu.CompilerParams(
-            collective_id=0, has_side_effects=True, vmem_limit_bytes=32 * 1024 * 1024
+            collective_id=0, has_side_effects=True, vmem_limit_bytes=60 * 1024 * 1024
         ),
-    )(velocity, turbine_frame, turbine_live, polar_bin, erosion_id, polar, erosion)
+    )(
+        velocity,
+        turbine_frame,
+        turbine_live,
+        jnp.transpose(polar_bin, (0, 2, 1, 3)),
+        erosion_id,
+        polar,
+        erosion,
+    )
+    return flow, jnp.transpose(load, (0, 3, 1, 2, 4))
 
 
 def solution(mesh):

time: 37 us -> 32.8 us (0.89)
  Pallas kernels: 32.5 us -> 29.1 us
  local copies, waits for them, and re-layouts: 3 us -> 2.3 us
    pallas_call x1, Pallas kernels: 32.5 us -> 29.1 us  [body(): pl.pallas_call(functools.partial(step_kernel, lax.axis_size('gx'), lax.ax...]
    pallas_call x1 -> x0, local copies, waits for them, and re-layouts: 0.61 us -> none  [body(): pl.pallas_call(functools.partial(step_kernel, lax.axis_size('gx'), lax.ax...]
    unnamed x12 -> x4, local copies, waits for them, and re-layouts: 2.39 us -> 2.3 us
where the time goes in v2:
time: 32.8 us; the launch traced here: 32.7 us
  Pallas kernels  29.1 us (89%)
  local copies, waits for them, and re-layouts  2.3 us (7%)
  between operations  1.29 us (4%)
    pallas_call x1, Pallas kernels, body(): pl.pallas_call(functools.partial(step_kernel, lax.axis_size('gx'), lax.ax...  29.1 us
    unnamed x4, local copies, waits for them, and re-layouts  2.3 us

profile of v2, /device:TPU:0, one launch (start us, length us, event | category | flops | bytes accessed | tf_op | source)
XLA Modules:
  0.0 32.7 jit_solution(6130298498018796355)
XLA Ops:
  1.3 29.1 %shard_map.86 = (f32[3,8,24,128]{3,2,1,0:T(8,128)}, f32[1,3,3,1,256]{4,3,2,1,0:T(1,128)}) custom-call(f32[3,8,24,128]{3,2,1,0:T(8,128)} %u_hbm.1, f32[1,1,4]{2,1,0:T(1,128)} %frame_hbm.1, s32[1,1,1]{2,1,0:T(1,128)S(6)} %copy.12.live_hbm, s32[1,3,1,256]{3,2,1,0:T(1,128)} %bitcast.5, s32[1,1,3]{2,1,0:T(1,128)} %wear_hbm.1, f32[5,8]{1,0:T(8,128)} %polar_hbm.1, ...), custom_call_target="tpu_custom_call" | custom-call | tf_op jit(solution)/shard_map/pallas_call | solution.py:523
  30.4 0.0 copy-start
  30.4 1.7 %copy.13 = f32[3,8,24,128]{3,2,1,0:T(8,128)} copy(f32[3,8,24,128]{3,2,1,0:T(8,128)} %get-tuple-element.10) | data formatting | bytes 589824
  32.1 0.0 copy-done
  32.1 0.6 %copy.14 = f32[1,1,3,3,256]{4,1,3,2,0:T(1,128)} copy(f32[1,1,3,3,256]{4,1,3,2,0:T(1,128)S(1)} %bitcast.4) | data formatting | bytes 18432
Async XLA Ops:
  30.4 1.7 %copy-start = (f32[1,3,3,1,256]{4,3,2,1,0:T(1,128)S(1)}, f32[1,3,3,1,256]{4,3,2,1,0:T(1,128)}, u32[]{:S(2)}) copy-start(f32[1,3,3,1,256]{4,3,2,1,0:T(1,128)} %get-tuple-element.5) | copy-start | bytes 27652

commit v3 on v2

--- a/solution.py
+++ b/solution.py
@@ -133,11 +133,11 @@
     me_x = lax.axis_index("gx")
     me_y = lax.axis_index("gy")
 
+    along_x = [lax.rem(me_x + (step + count_x), count_x) for step in (-1, 0, 1)]
+    along_y = [lax.rem(me_y + (step + count_y), count_y) for step in (-1, 0, 1)]
+
     def neighbour(offset):
-        return {
-            "gx": lax.rem(me_x + (offset[0] + count_x), count_x),
-            "gy": lax.rem(me_y + (offset[1] + count_y), count_y),
-        }
+        return {"gx": along_x[offset[0] + 1], "gy": along_y[offset[1] + 1]}
 
     def send(src, dst, sems, target, source_slot, target_slot):
         copy = pltpu.make_async_remote_copy(
@@ -262,7 +262,8 @@
         cells_y = lax.broadcasted_iota(jnp.int32, (width, 1), 0).astype(F32) - MARGIN
         wy_ref[substep] = phi(cells_y - y_point)
         cells_z = depth_start + lax.broadcasted_iota(jnp.int32, (DEPTH, 1), 0).astype(F32)
-        wz_ref[substep] = phi(cells_z - z_point).astype(BF16)
+        depth = phi(cells_z - z_point).astype(BF16)
+        wz_ref[substep] = jnp.concatenate([depth, depth], axis=0)
 
     point_weights(0)
 
@@ -447,8 +448,8 @@
             window = window + rows_ref[substep, slot(offset)]
         sent += list(row_copies.values())
         high, low = halves(window)
-        wz = wz_ref[substep]
-        column = dot(high, wz, 0, 0) + dot(low, wz, 0, 0)
+        column = dot(jnp.concatenate([high, low], axis=0), wz_ref[substep], 0, 0)
+        wz = wz_ref[substep, 0:DEPTH, :]
         wy = wy_ref[substep]
         velocity = [
             jnp.sum(column[c * width : (c + 1) * width] * wy, axis=0, keepdims=True)
@@ -541,7 +542,7 @@
             pltpu.VMEM((turbines, brick_x, LANES), F32),
             pltpu.VMEM((turbines, 2 * DEPTH, height), BF16),
             pltpu.VMEM((STEPS, width, POINTS), F32),
-            pltpu.VMEM((STEPS, DEPTH, POINTS), BF16),
+            pltpu.VMEM((STEPS, 2 * DEPTH, POINTS), BF16),
             pltpu.VMEM((comps, brick_x, brick_y, height), F32),
             pltpu.VMEM((turbines, LANES, height), F32),
             pltpu.SMEM(turbine_frame.shape, F32),
@@ -558,7 +559,7 @@
             pltpu.SemaphoreType.DMA((STEPS, 2, 2)),
         ],
         compiler_params=pltpu.CompilerParams(
-            collective_id=0, has_side_effects=True, vmem_limit_bytes=60 * 1024 * 1024
+            collective_id=0, has_side_effects=True, vmem_limit_bytes=54 * 1024 * 1024
         ),
     )(
         velocity,

time: 32.8 us -> 32.5 us (level)
  Pallas kernels: 29.1 us -> 28.7 us
    pallas_call x1, Pallas kernels: 29.1 us -> 28.7 us  [body(): pl.pallas_call(functools.partial(step_kernel, lax.axis_size('gx'), lax.ax...]
where the time goes in v3:
time: 32.5 us; the launch traced here: 32.3 us
  Pallas kernels  28.7 us (88%)
  local copies, waits for them, and re-layouts  2.3 us (7%)
  between operations  1.29 us (4%)
    pallas_call x1, Pallas kernels, body(): pl.pallas_call(functools.partial(step_kernel, lax.axis_size('gx'), lax.ax...  28.7 us
    unnamed x4, local copies, waits for them, and re-layouts  2.3 us

profile of v3, /device:TPU:0, one launch (start us, length us, event | category | flops | bytes accessed | tf_op | source)
XLA Modules:
  0.0 32.3 jit_solution(16296364333992351497)
XLA Ops:
  1.3 28.7 %shard_map.86 = (f32[3,8,24,128]{3,2,1,0:T(8,128)}, f32[1,3,3,1,256]{4,3,2,1,0:T(1,128)}) custom-call(f32[3,8,24,128]{3,2,1,0:T(8,128)} %u_hbm.1, f32[1,1,4]{2,1,0:T(1,128)} %frame_hbm.1, s32[1,1,1]{2,1,0:T(1,128)S(6)} %copy.12.live_hbm, s32[1,3,1,256]{3,2,1,0:T(1,128)} %bitcast.5, s32[1,1,3]{2,1,0:T(1,128)} %wear_hbm.1, f32[5,8]{1,0:T(8,128)} %polar_hbm.1, ...), custom_call_target="tpu_custom_call" | custom-call | tf_op jit(solution)/shard_map/pallas_call | solution.py:524
  30.0 0.0 copy-start
  30.0 1.7 %copy.13 = f32[3,8,24,128]{3,2,1,0:T(8,128)} copy(f32[3,8,24,128]{3,2,1,0:T(8,128)} %get-tuple-element.10) | data formatting | bytes 589824
  31.7 0.0 copy-done
  31.7 0.6 %copy.14 = f32[1,1,3,3,256]{4,1,3,2,0:T(1,128)} copy(f32[1,1,3,3,256]{4,1,3,2,0:T(1,128)S(1)} %bitcast.4) | data formatting | bytes 18432
Async XLA Ops:
  30.0 1.7 %copy-start = (f32[1,3,3,1,256]{4,3,2,1,0:T(1,128)S(1)}, f32[1,3,3,1,256]{4,3,2,1,0:T(1,128)}, u32[]{:S(2)}) copy-start(f32[1,3,3,1,256]{4,3,2,1,0:T(1,128)} %get-tuple-element.5) | copy-start | bytes 27652
